TPU v7x, 512 devices: a whole 4x4x16 slice. The times are simulated.
512 devices in a mesh: dp: 32 (over z_lo, x, core), mp: 16 (over z_hi, y).
Axes of the slice: x: 4, y: 4, z: 16 (z_hi: 4, z_lo: 4; z = z_hi * 4 + z_lo), core: 2. Of those that a mesh axis runs over, the one named last changes fastest.
Arguments:
- grads: bfloat16 [32, 2, 256, 28672], P('dp', None, None, 'mp'), may hold values from -6 to 6
- weights: bfloat16 [2, 256, 28672], P(None, 'dp', 'mp'), may hold values from -1.5 to 1.5
- first_moment: float32 [2, 256, 256], P(None, 'dp'), may hold values from -6 to 6
- second_moment: float32 [2, 256, 256], P(None, 'dp'), may hold values from 1 to 16
- old_seeds: int32 [2], replicated, may hold values from 0 to 999999
- new_seeds: int32 [2], replicated, may hold values from 0 to 999999
Outputs:
- new_weights: bfloat16 [2, 256, 28672], P(None, None, 'mp')
- new_first: float32 [2, 256, 256], P(None, 'dp')
- new_second: float32 [2, 256, 256], P(None, 'dp')
Inputs may be any that keep to these rules, and one draw needn't show every extreme that they name: `old_seeds`: seeds of the counter-based generator; old and new seeds are drawn independently. `new_seeds`: seeds of the counter-based generator; old and new seeds are drawn independently.
All inputs are finite; a program needn't handle non-finite values.
Results may differ from a plain program's by a relative error of at most 0.0053.
Values may be sent and summed in bfloat16 or wider, within the bound.
No kernel may reach another device: no remote copies, remote signals or barrier semaphores. Data moves between devices by JAX's collectives and lax.ppermute only.
A program may use at most 64 MiB of HBM per device.

v0:
```python
import math
import jax
import jax.numpy as jnp
from jax import lax
from jax.sharding import PartitionSpec as P


def scramble(values):
    return (values % 46000 * (values // 2 % 46000 + 1) + 12345) % 65521


def generate(seed_value, rank_ids, columns):
    offset = seed_value % 65521
    row_key = (rank_ids * 251 + offset * 3) % 65521
    col_key = scramble((columns * 7 + offset) % 65521)
    hashed = scramble((row_key[:, None] + 2 * col_key[None, :]) % 65521)
    hashed = scramble((hashed * 3 + row_key[:, None]) % 65521)
    spread = math.sqrt(12.0 / rank_ids.shape[0])
    return ((hashed.astype(jnp.float32) + 0.5) / 65521.0 - 0.5) * spread


def inner_rank(left, right):
    return lax.dot_general(
        left, right, (((1,), (1,)), ((), ())), preferred_element_type=jnp.float32
    )


def shards(grads, weights, first_moment, second_moment, old_seeds, new_seeds):
    layers = weights.shape[0]
    rank = first_moment.shape[2]
    ncols = weights.shape[2]
    col_start = lax.axis_index("mp") * ncols
    columns = col_start + jnp.arange(ncols, dtype=jnp.int32)
    rank_ids = jnp.arange(rank, dtype=jnp.int32)
    new_projs = [
        generate(new_seeds[layer_id], rank_ids, columns).astype(jnp.bfloat16)
        for layer_id in range(layers)
    ]
    gathered = []
    firsts = []
    seconds = []
    for layer_id in range(layers):
        new_proj = new_projs[layer_id]
        old_proj = generate(old_seeds[layer_id], rank_ids, columns).astype(jnp.bfloat16)
        gram_matrix = lax.psum(inner_rank(old_proj, new_proj), "mp")
        partial_value = inner_rank(grads[0, layer_id], new_proj)
        owned = lax.psum_scatter(partial_value, "dp", scatter_dimension=0, tiled=True)
        compressed = lax.psum(owned, "mp")
        moment = (
            0.9 * jnp.dot(first_moment[layer_id], gram_matrix, precision=lax.Precision.HIGHEST)
            + 0.1 * compressed
        )
        second = (
            0.95
            * jnp.dot(
                second_moment[layer_id], gram_matrix * gram_matrix, precision=lax.Precision.HIGHEST
            )
            + 0.05 * compressed * compressed
        )
        direction = (moment / (jnp.sqrt(second) + 1e-08)).astype(jnp.bfloat16)
        update = jnp.dot(direction, new_proj, preferred_element_type=jnp.float32)
        block = (weights[layer_id].astype(jnp.float32) - 0.5 * update).astype(jnp.bfloat16)
        gathered.append(lax.all_gather(block, "dp", axis=0, tiled=True))
        firsts.append(moment)
        seconds.append(second)
    new_weights = jnp.stack(gathered)
    return (new_weights, jnp.stack(firsts), jnp.stack(seconds))


def solution(mesh):
    placed = (
        P("dp", None, None, "mp"),
        P(None, "dp", "mp"),
        P(None, "dp", None),
        P(None, "dp", None),
        P(),
        P(),
    )
    return jax.shard_map(
        shards,
        mesh=mesh,
        in_specs=placed,
        out_specs=(P(None, None, "mp"), P(None, "dp", None), P(None, "dp", None)),
        check_vma=False,
    )
```

profile of v0, /device:TPU:1, one launch (start us, length us, event | category | flops | bytes accessed | tf_op | source)
XLA Modules:
  0.0 542.0 jit_solution(2791521066732754462)
XLA Ops:
  8.0 0.0 reduce-scatter.5.cloned.1.call-start
  8.0 1.3 fusion.313
  10.1 11.9 %convolution_bitcast_fusion = f32[256,256]{1,0:T(8,128)} fusion(bf16[1,2,256,1792]{3,2,1,0:T(8,128)(2,1)} %param.6, s32[1792]{0:T(1024)S(1)} %fusion.205, s32[256]{0:T(256)S(1)} %and_select_fusion), kind=kOutput, calls=%fused_computation.211 | convolution fusion | flops 277544960 | bytes 1187840 | tf_op jit(solution)/shard_map/dot_general | solution.py:23
  22.1 0.3 reduce-scatter.3.cloned.1.call-start
  23.1 10.6 %convolution_bitcast_fusion.1 = f32[256,256]{1,0:T(8,128)} fusion(bf16[1,2,256,1792]{3,2,1,0:T(8,128)(2,1)S(1)} %copy-done.3, s32[1792]{0:T(1024)S(1)} %fusion.191, s32[256]{0:T(256)S(1)} %and_select_fusion.2), kind=kOutput, calls=%fused_computation.212 | convolution fusion | flops 277544960 | bytes 1188864 | tf_op jit(solution)/shard_map/dot_general | solution.py:23
  33.8 0.4 all-reduce.4.cloned.1.call-start
  34.2 0.6 fusion.312
  36.1 0.1 fusion.184
  36.2 20.4 %fusion.138 = f32[256,256]{1,0:T(8,128)} fusion(s32[1792]{0:T(1024)S(1)} %fusion.191, s32[256]{0:T(256)S(1)} %and_select_fusion.2, s32[1792]{0:T(1024)S(1)} %get-tuple-element.11, s32[256]{0:T(256)S(1)} %and_select_fusion.3), kind=kOutput, calls=%fused_computation.226 | convolution fusion | flops 320208896 | bytes 278528 | tf_op jit(solution)/shard_map/dot_general | solution.py:23
  56.7 20.8 %fusion.136 = f32[256,256]{1,0:T(8,128)} fusion(s32[1792]{0:T(1024)S(1)} %get-tuple-element.12, s32[256]{0:T(256)S(1)} %and_select_fusion.1, s32[1792]{0:T(1024)S(1)} %fusion.205, s32[256]{0:T(256)S(1)} %and_select_fusion), kind=kOutput, calls=%fused_computation.225 | convolution fusion | flops 320208896 | bytes 278528 | tf_op jit(solution)/shard_map/dot_general | solution.py:23
  77.5 95.8 %reduce-scatter.5.cloned.1.call-done = f32[8,256]{1,0:T(8,128)} async-done(((f32[256,256]{1,0:T(8,128)}), f32[8,256]{1,0:T(8,128)}) %reduce-scatter.5.cloned.1.call-update) | async-done | bytes 8208 | tf_op jit(solution)/shard_map/reduce_scatter | solution.py:47
  173.4 149.7 %reduce-scatter.3.cloned.1.call-done = f32[8,256]{1,0:T(8,128)} async-done(((f32[256,256]{1,0:T(8,128)}), f32[8,256]{1,0:T(8,128)}) %reduce-scatter.3.cloned.1.call-update) | async-done | bytes 8208 | tf_op jit(solution)/shard_map/reduce_scatter | solution.py:47
  323.1 84.7 %all-reduce = (f32[8,256]{1,0:T(8,128)S(1)}, f32[8,256]{1,0:T(8,128)S(1)}) all-reduce(f32[8,256]{1,0:T(8,128)} %reduce-scatter.5.cloned.1.call-done, f32[8,256]{1,0:T(8,128)} %reduce-scatter.3.cloned.1.call-done), channel_id=1, replica_groups=mesh['dp'=32,'mp'=16] {'mp'}, use_global_device_ids=true, to_apply=%region_5.6 | all-reduce | flops 4096 | bytes 32768 | tf_op jit(solution)/shard_map/psum | solution.py:48
  407.8 1.2 fusion.129
  409.0 1.2 fusion.131
  410.1 1.2 fusion.133
  411.4 1.2 fusion.135
  412.6 9.8 %fusion.3 = bf16[8,1792]{1,0:T(8,128)(2,1)S(1)} fusion(s32[1792]{0:T(1024)S(1)} %fusion.205, s32[256]{0:T(256)S(1)} %and_select_fusion, bf16[2,8,1792]{2,1,0:T(8,128)(2,1)S(1)} %copy-done.4, f32[8,256]{1,0:T(8,128)S(1)} %fusion.131, f32[8,256]{1,0:T(8,128)S(1)} %fusion.129), kind=kOutput, calls=%fused_computation.69 | convolution fusion | flops 50067456 | bytes 81920 | tf_op jit(solution)/shard_map/dot_general | solution.py:61
  422.4 57.5 %all_gather.7 = bf16[256,1792]{1,0:T(8,128)(2,1)S(1)} all-gather(bf16[8,1792]{1,0:T(8,128)(2,1)S(1)} %fusion.3), channel_id=1, replica_groups=mesh['dp'=32,'mp'=16] {'dp'}, dimensions={0}, use_global_device_ids=true | all-gather | bytes 946176 | tf_op jit(solution)/shard_map/all_gather | solution.py:63
  479.9 9.8 %fusion.2 = bf16[8,1792]{1,0:T(8,128)(2,1)S(1)} fusion(s32[1792]{0:T(1024)S(1)} %fusion.191, s32[256]{0:T(256)S(1)} %and_select_fusion.2, bf16[2,8,1792]{2,1,0:T(8,128)(2,1)S(1)} %copy-done.4, f32[8,256]{1,0:T(8,128)S(1)} %fusion.135, f32[8,256]{1,0:T(8,128)S(1)} %fusion.133), kind=kOutput, calls=%fused_computation.68 | convolution fusion | flops 50067456 | bytes 81920 | tf_op jit(solution)/shard_map/dot_general | solution.py:61
  489.7 41.9 %all_gather.6 = bf16[256,1792]{1,0:T(8,128)(2,1)S(1)} all-gather(bf16[8,1792]{1,0:T(8,128)(2,1)S(1)} %fusion.2), channel_id=1, replica_groups=mesh['dp'=32,'mp'=16] {'dp'}, dimensions={0}, use_global_device_ids=true | all-gather | bytes 946176 | tf_op jit(solution)/shard_map/all_gather | solution.py:63
  531.6 0.6 pad_maximum_fusion.2
  532.2 0.6 pad_maximum_fusion.1
  532.8 1.4 pad_maximum_fusion
  (20 shorter events, 0.3 us)
Async XLA Ops:
  8.0 165.4 %reduce-scatter.5.cloned.1.call-start = ((), (), s32[]{:S(2)}) async-start(), calls=%async_computation.3 | async-start | bytes 270336 | tf_op jit(solution)/shard_map/reduce_scatter | solution.py:47
  10.1 13.0 %copy-start.3 = (bf16[1,2,256,1792]{3,2,1,0:T(8,128)(2,1)S(1)}, bf16[1,2,256,1792]{3,2,1,0:T(8,128)(2,1)}, u32[]{:S(2)}) copy-start(bf16[1,2,256,1792]{3,2,1,0:T(8,128)(2,1)} %param.6) | copy-start | bytes 5505028
  22.1 301.0 %reduce-scatter.3.cloned.1.call-start = ((), (), s32[]{:S(2)}) async-start(), calls=%async_computation.2 | async-start | bytes 270336 | tf_op jit(solution)/shard_map/reduce_scatter | solution.py:47
  23.1 11.1 %copy-start.2 = (s32[2]{0:T(128)S(1)}, s32[2]{0:T(128)}, u32[]{:S(2)}) copy-start(s32[2]{0:T(128)} %param.10) | copy-start | bytes 28
  33.8 374.0 %all-reduce.4.cloned.1.call-start = ((), (), s32[]{:S(2)}) async-start(), calls=%async_computation.4 | async-start | bytes 1048576 | tf_op jit(solution)/shard_map/psum | solution.py:45
  56.7 351.1 %copy-start = (f32[2,8,256]{2,1,0:T(8,128)S(1)}, f32[2,8,256]{2,1,0:T(8,128)}, u32[]{:S(2)}) copy-start(f32[2,8,256]{2,1,0:T(8,128)} %param.9) | copy-start | bytes 49156
  56.7 352.3 %copy-start.1 = (f32[2,8,256]{2,1,0:T(8,128)S(1)}, f32[2,8,256]{2,1,0:T(8,128)}, u32[]{:S(2)}) copy-start(f32[2,8,256]{2,1,0:T(8,128)} %param.8) | copy-start | bytes 49156
  56.7 355.9 %copy-start.4 = (bf16[2,8,1792]{2,1,0:T(8,128)(2,1)S(1)}, bf16[2,8,1792]{2,1,0:T(8,128)(2,1)}, u32[]{:S(2)}) copy-start(bf16[2,8,1792]{2,1,0:T(8,128)(2,1)} %param.7) | copy-start | bytes 172036
Sparse Core Ops, SparseCore 0:
  22.2 151.1 reduce-scatter.4
  176.1 146.8 reduce-scatter.2
Sparse Core Ops, SparseCore 1:
  77.6 199.6 all-reduce.3
where the time goes:
time: 550 us; the launch traced here: 542 us
  waiting for transfers between devices  246 us (45%)
  blocking collectives  184 us (33%)
  matrix products  88.2 us (16%)
  between operations  18.6 us (3%)
    reduce_scatter x2, waiting for transfers between devices, shards(): lax.psum_scatter(partial_value, 'dp', scatter_dimension=0, tiled=True)  246 us
    all_gather x2, blocking collectives, shards(): gathered.append(lax.all_gather(block, 'dp', axis=0, tiled=True))  99.4 us
    psum x1, blocking collectives, shards(): compressed = lax.psum(owned, 'mp')  84.7 us
    dot_general x4, matrix products, inner_rank(): lax.dot_general(left, right, (((1,), (1,)), ((), ())), preferred_element_...  63.8 us
    dot_general x2, matrix products, shards(): update = jnp.dot(direction, new_proj, preferred_element_type=jnp.float32)  19.6 us
  transfers between devices with their start and end apart: 3, of which 2 were waited for; matrix products, arithmetic and copies ran while one was open for 10% of the time, Pallas kernels for 0%

commit v1 on v0

--- a/solution.py
+++ b/solution.py
@@ -45,7 +45,7 @@
         gram_matrix = lax.psum(inner_rank(old_proj, new_proj), "mp")
         partial_value = inner_rank(grads[0, layer_id], new_proj)
         owned = lax.psum_scatter(partial_value, "dp", scatter_dimension=0, tiled=True)
-        compressed = lax.psum(owned, "mp")
+        compressed = jnp.sum(lax.all_gather(owned, "mp"), axis=0)
         moment = (
             0.9 * jnp.dot(first_moment[layer_id], gram_matrix, precision=lax.Precision.HIGHEST)
             + 0.1 * compressed

time: 550 us -> 505 us (0.918)
  waiting for transfers between devices: 246 us -> 197 us
    all_gather x0 -> x2, blocking collectives: none -> 94.5 us  [shards(): compressed = jnp.sum(lax.all_gather(owned, 'mp'), axis=0)]
    reduce_scatter x2, waiting for transfers between devices: 246 us -> 154 us  [shards(): lax.psum_scatter(partial_value, 'dp', scatter_dimension=0, tiled=True)]
    psum x1 -> x0, blocking collectives: 84.7 us -> none  [shards(): compressed = lax.psum(owned, 'mp')]
    psum x1, waiting for transfers between devices: 0.01 us -> 43 us  [shards(): gram_matrix = lax.psum(inner_rank(old_proj, new_proj), 'mp')]
    all_gather x2, blocking collectives: 99.4 us -> 92.8 us  [shards(): gathered.append(lax.all_gather(block, 'dp', axis=0, tiled=True))]
  transfers between devices with their start and end apart: 3 -> 3, of which waited for: 2 -> 3; matrix products, arithmetic and copies ran while one was open for 10% -> 11% of each run, Pallas kernels for 0% -> 0%
where the time goes in v1:
time: 505 us; the launch traced here: 497 us
  waiting for transfers between devices  197 us (39%)
  blocking collectives  187 us (37%)
  matrix products  86.6 us (17%)
  between operations  18.5 us (4%)
    reduce_scatter x2, waiting for transfers between devices, shards(): lax.psum_scatter(partial_value, 'dp', scatter_dimension=0, tiled=True)  154 us
    all_gather x2, blocking collectives, shards(): compressed = jnp.sum(lax.all_gather(owned, 'mp'), axis=0)  94.5 us
    all_gather x2, blocking collectives, shards(): gathered.append(lax.all_gather(block, 'dp', axis=0, tiled=True))  92.8 us
    dot_general x4, matrix products, inner_rank(): lax.dot_general(left, right, (((1,), (1,)), ((), ())), preferred_element_...  62.3 us
    psum x1, waiting for transfers between devices, shards(): gram_matrix = lax.psum(inner_rank(old_proj, new_proj), 'mp')  43 us
    dot_general x2, matrix products, shards(): update = jnp.dot(direction, new_proj, preferred_element_type=jnp.float32)  19.6 us
  transfers between devices with their start and end apart: 3, of which 3 were waited for; matrix products, arithmetic and copies ran while one was open for 11% of the time, Pallas kernels for 0%

profile of v1, /device:TPU:1, one launch (start us, length us, event | category | flops | bytes accessed | tf_op | source)
XLA Modules:
  0.0 497.0 jit_solution(18124603267146385812)
XLA Ops:
  8.0 1.3 fusion.312
  10.0 1.4 fusion.313
  12.2 11.1 %convolution_bitcast_fusion = f32[256,256]{0,1:T(8,128)S(1)} fusion(bf16[1,2,256,1792]{3,2,1,0:T(8,128)(2,1)} %param.6, s32[1792]{0:T(1024)S(1)} %get-tuple-element.12, s32[256]{0:T(256)S(1)} %get-tuple-element.13), kind=kOutput, calls=%fused_computation.211 | convolution fusion | flops 277544960 | bytes 1187840 | tf_op jit(solution)/shard_map/dot_general | solution.py:23
  23.3 0.8 copy.15
  25.8 20.5 %fusion.136 = f32[256,256]{1,0:T(8,128)} fusion(s32[1792]{0:T(1024)S(1)} %get-tuple-element.11, s32[256]{0:T(256)S(1)} %get-tuple-element.14, s32[1792]{0:T(1024)S(1)} %get-tuple-element.12, s32[256]{0:T(256)S(1)} %get-tuple-element.13), kind=kOutput, calls=%fused_computation.225 | convolution fusion | flops 320208896 | bytes 278528 | tf_op jit(solution)/shard_map/dot_general | solution.py:23
  46.3 20.9 %fusion.138 = f32[256,256]{1,0:T(8,128)} fusion(s32[1792]{0:T(1024)S(1)} %get-tuple-element.10, s32[256]{0:T(256)S(1)} %get-tuple-element.15, s32[1792]{0:T(1024)S(1)} %get-tuple-element.9, s32[256]{0:T(256)S(1)} %get-tuple-element.16), kind=kOutput, calls=%fused_computation.226 | convolution fusion | flops 320208896 | bytes 278528 | tf_op jit(solution)/shard_map/dot_general | solution.py:23
  67.3 9.9 %convolution_bitcast_fusion.1 = f32[256,256]{0,1:T(8,128)S(1)} fusion(bf16[1,2,256,1792]{3,2,1,0:T(8,128)(2,1)S(1)} %copy-done.2, s32[1792]{0:T(1024)S(1)} %get-tuple-element.10, s32[256]{0:T(256)S(1)} %get-tuple-element.15), kind=kOutput, calls=%fused_computation.212 | convolution fusion | flops 277544960 | bytes 1188864 | tf_op jit(solution)/shard_map/dot_general | solution.py:23
  77.2 0.8 copy.13
  78.1 97.5 %reduce-scatter.9.cloned.1.call-done = f32[8,256]{1,0:T(8,128)} async-done(((f32[256,256]{1,0:T(8,128)}), f32[8,256]{1,0:T(8,128)}) %reduce-scatter.9.cloned.1.call-update) | async-done | bytes 8208 | tf_op jit(solution)/shard_map/reduce_scatter | solution.py:47
  175.6 48.2 %all-gather.1 = f32[128,256]{1,0:T(8,128)S(1)} all-gather(f32[8,256]{1,0:T(8,128)} %reduce-scatter.9.cloned.1.call-done), channel_id=3, replica_groups=mesh['dp'=32,'mp'=16] {'mp'}, dimensions={0}, use_global_device_ids=true | all-gather | bytes 139264 | tf_op jit(solution)/shard_map/all_gather | solution.py:48
  223.8 43.0 %all-reduce.3.cloned.1.call-done = (f32[256,256]{1,0:T(8,128)}, f32[256,256]{1,0:T(8,128)}) async-done(((f32[256,256]{1,0:T(8,128)}, f32[256,256]{1,0:T(8,128)}), (f32[256,256]{1,0:T(8,128)}, f32[256,256]{1,0:T(8,128)})) %all-reduce.3.cloned.1.call-update) | async-done | bytes 524304 | tf_op jit(solution)/shard_map/psum | solution.py:45
  266.8 1.2 fusion.129
  268.0 1.2 fusion.131
  269.2 56.3 %reduce-scatter.7.cloned.1.call-done = f32[8,256]{1,0:T(8,128)} async-done(((f32[256,256]{1,0:T(8,128)}), f32[8,256]{1,0:T(8,128)}) %reduce-scatter.7.cloned.1.call-update) | async-done | bytes 8208 | tf_op jit(solution)/shard_map/reduce_scatter | solution.py:47
  325.5 46.3 %all-gather = f32[128,256]{1,0:T(8,128)S(1)} all-gather(f32[8,256]{1,0:T(8,128)} %reduce-scatter.7.cloned.1.call-done), channel_id=2, replica_groups=mesh['dp'=32,'mp'=16] {'mp'}, dimensions={0}, use_global_device_ids=true | all-gather | bytes 139264 | tf_op jit(solution)/shard_map/all_gather | solution.py:48
  371.9 1.2 fusion.133
  373.1 1.2 fusion.135
  374.3 9.8 %fusion.2 = bf16[8,1792]{1,0:T(8,128)(2,1)S(1)} fusion(s32[1792]{0:T(1024)S(1)} %get-tuple-element.10, s32[256]{0:T(256)S(1)} %get-tuple-element.15, bf16[2,8,1792]{2,1,0:T(8,128)(2,1)S(1)} %copy-done.3, f32[8,256]{1,0:T(8,128)S(1)} %fusion.135, f32[8,256]{1,0:T(8,128)S(1)} %fusion.133), kind=kOutput, calls=%fused_computation.68 | convolution fusion | flops 50067456 | bytes 81920 | tf_op jit(solution)/shard_map/dot_general | solution.py:61
  384.1 50.9 %all_gather.20 = bf16[256,1792]{1,0:T(8,128)(2,1)S(1)} all-gather(bf16[8,1792]{1,0:T(8,128)(2,1)S(1)} %fusion.2), channel_id=1, replica_groups=mesh['dp'=32,'mp'=16] {'dp'}, dimensions={0}, use_global_device_ids=true | all-gather | bytes 946176 | tf_op jit(solution)/shard_map/all_gather | solution.py:63
  435.1 9.8 %fusion.3 = bf16[8,1792]{1,0:T(8,128)(2,1)S(1)} fusion(s32[1792]{0:T(1024)S(1)} %get-tuple-element.12, s32[256]{0:T(256)S(1)} %get-tuple-element.13, bf16[2,8,1792]{2,1,0:T(8,128)(2,1)S(1)} %copy-done.3, f32[8,256]{1,0:T(8,128)S(1)} %fusion.131, f32[8,256]{1,0:T(8,128)S(1)} %fusion.129), kind=kOutput, calls=%fused_computation.69 | convolution fusion | flops 50067456 | bytes 81920 | tf_op jit(solution)/shard_map/dot_general | solution.py:61
  444.9 41.9 %all_gather.23 = bf16[256,1792]{1,0:T(8,128)(2,1)S(1)} all-gather(bf16[8,1792]{1,0:T(8,128)(2,1)S(1)} %fusion.3), channel_id=1, replica_groups=mesh['dp'=32,'mp'=16] {'dp'}, dimensions={0}, use_global_device_ids=true | all-gather | bytes 946176 | tf_op jit(solution)/shard_map/all_gather | solution.py:63
  486.8 0.6 pad_maximum_fusion.2
  487.4 0.6 pad_maximum_fusion.1
  488.0 1.4 pad_maximum_fusion
  (20 shorter events, 0.6 us)
Async XLA Ops:
  8.0 167.6 %reduce-scatter.9.cloned.1.call-start = ((), (), s32[]{:S(2)}) async-start(), calls=%async_computation.3 | async-start | bytes 270336 | tf_op jit(solution)/shard_map/reduce_scatter | solution.py:47
  24.2 242.6 %all-reduce.3.cloned.1.call-start = ((), (), s32[]{:S(2)}) async-start(), calls=%async_computation.4 | async-start | bytes 1048576 | tf_op jit(solution)/shard_map/psum | solution.py:45
  46.3 21.0 %copy-start.2 = (bf16[1,2,256,1792]{3,2,1,0:T(8,128)(2,1)S(1)}, bf16[1,2,256,1792]{3,2,1,0:T(8,128)(2,1)}, u32[]{:S(2)}) copy-start(bf16[1,2,256,1792]{3,2,1,0:T(8,128)(2,1)} %param.6) | copy-start | bytes 5505028
  67.2 199.6 %copy-start = (f32[2,8,256]{2,1,0:T(8,128)S(1)}, f32[2,8,256]{2,1,0:T(8,128)}, u32[]{:S(2)}) copy-start(f32[2,8,256]{2,1,0:T(8,128)} %param.9) | copy-start | bytes 49156
  67.2 200.8 %copy-start.1 = (f32[2,8,256]{2,1,0:T(8,128)S(1)}, f32[2,8,256]{2,1,0:T(8,128)}, u32[]{:S(2)}) copy-start(f32[2,8,256]{2,1,0:T(8,128)} %param.8) | copy-start | bytes 49156
  67.2 258.3 %reduce-scatter.7.cloned.1.call-start = ((), (), s32[]{:S(2)}) async-start(), calls=%async_computation.2 | async-start | bytes 270336 | tf_op jit(solution)/shard_map/reduce_scatter | solution.py:47
  77.2 297.1 %copy-start.3 = (bf16[2,8,1792]{2,1,0:T(8,128)(2,1)S(1)}, bf16[2,8,1792]{2,1,0:T(8,128)(2,1)}, u32[]{:S(2)}) copy-start(bf16[2,8,1792]{2,1,0:T(8,128)(2,1)} %param.7) | copy-start | bytes 172036
Sparse Core Ops, SparseCore 0:
  24.3 151.2 reduce-scatter.8
  178.4 147.1 reduce-scatter.6
Sparse Core Ops, SparseCore 1:
  67.3 199.5 all-reduce.2
